TPU v7x, 32 devices: a whole 2x2x4 slice. The times are simulated.
32 devices in a mesh: samp: 8 (over z, y), col: 4 (over x, core).
Axes of the slice: x: 2, y: 2, z: 4, core: 2. Of those that a mesh axis runs over, the one named last changes fastest.
Arguments:
- spectra: float32 [16384, 8192], P('samp', 'col'), as said below
- w_start: float32 [16384, 512], P('samp'), may hold values from 0.05 to 1
- h_start: float32 [8192, 512], P('col'), may hold values from 0.05 to 1
Outputs:
- w_factor: float32 [16384, 512], P('samp')
- h_factor: float32 [8192, 512], P('col')
Inputs may be any that keep to these rules, and one draw needn't show every extreme that they name: `spectra`: every entry is positive.
All inputs are finite; a program needn't handle non-finite values.
Results may differ from a plain program's by a relative error of at most 0.0003.
Values sent between devices are 32-bit elements; how exact they have to be, the bound alone decides.
A program may use at most 128 MiB of HBM per device.

v0:
```python
import jax
import jax.numpy as jnp
from jax import lax
from jax.sharding import PartitionSpec as P

BLOCK = 128
SWEEPS = 3


floor_value = 1e-06


def sweep_factor(factor, product, gram_matrix):
    rank_width = gram_matrix.shape[0]
    for sweep_index in range(SWEEPS):
        for offset in range(0, rank_width, BLOCK):
            gram_cols = gram_matrix[:, offset : offset + BLOCK]
            majorant = jnp.sum(
                gram_matrix[offset : offset + BLOCK, offset : offset + BLOCK], axis=1
            )
            update = product[:, offset : offset + BLOCK] - jnp.dot(
                factor,
                gram_cols,
                precision=lax.Precision.HIGHEST,
                preferred_element_type=jnp.float32,
            )
            new_block = jnp.maximum(
                factor[:, offset : offset + BLOCK] + update / majorant, floor_value
            )
            factor = lax.dynamic_update_slice_in_dim(factor, new_block, offset, 1)
    return factor


def contract_rows(left, right):
    return lax.dot_general(
        left,
        right,
        (((0,), (0,)), ((), ())),
        precision=lax.Precision.HIGHEST,
        preferred_element_type=jnp.float32,
    )


def shards(spectra, w_start, h_start):
    gram_h_local = contract_rows(h_start, h_start)
    prod_local = jnp.dot(
        spectra, h_start, precision=lax.Precision.HIGHEST, preferred_element_type=jnp.float32
    )
    prod_w, gram_h = lax.psum((prod_local, gram_h_local), "col")
    w_factor = sweep_factor(w_start, prod_w, gram_h)
    gram_w_local = contract_rows(w_factor, w_factor)
    prod_local_h = contract_rows(spectra, w_factor)
    prod_h, gram_w = lax.psum((prod_local_h, gram_w_local), "samp")
    h_factor = sweep_factor(h_start, prod_h, gram_w)
    return (w_factor, h_factor)


def solution(mesh):
    return jax.shard_map(
        shards,
        mesh=mesh,
        in_specs=(P("samp", "col"), P("samp", None), P("col", None)),
        out_specs=(P("samp", None), P("col", None)),
        check_vma=False,
    )
```

profile of v0, /device:TPU:0, one launch (start us, length us, event | category | flops | bytes accessed | tf_op | source)
XLA Modules:
  0.0 487.0 jit_solution(15645905206511805387)
XLA Ops:
  12.7 8.0 %fusion.99 = f32[512,512]{1,0:T(8,128)} fusion(f32[2048,512]{1,0:T(8,128)S(1)} %copy.42), kind=kOutput, calls=%fused_computation.156 | convolution fusion | flops 6442450944 | bytes 5242880 | tf_op jit(solution)/shard_map/dot_general | solution.py:35
  20.7 28.3 %fusion.98 = f32[2048,512]{1,0:T(8,128)} fusion(f32[2048,2048]{1,0:T(8,128)S(1)} %copy-done.10, f32[2048,512]{1,0:T(8,128)S(1)} %copy.42), kind=kOutput, calls=%fused_computation.155 | convolution fusion | flops 25769803776 | bytes 25165824 | tf_op jit(solution)/shard_map/dot_general | solution.py:46
  49.6 105.0 %all-reduce.7.cloned.1.call-done = (f32[2048,512]{1,0:T(8,128)}, f32[512,512]{1,0:T(8,128)}) async-done(((f32[2048,512]{1,0:T(8,128)}, f32[512,512]{1,0:T(8,128)}), (f32[2048,512]{1,0:T(8,128)}, f32[512,512]{1,0:T(8,128)})) %all-reduce.7.cloned.1.call-update) | async-done | bytes 5242896 | tf_op jit(solution)/shard_map/psum | solution.py:49
  155.8 6.7 %fusion.73 = f32[2048,128]{1,0:T(8,128)S(1)} fusion(f32[2048,512]{1,0:T(8,128)} %copy.41, f32[2048,512]{1,0:T(8,128)} %get-tuple-element.12, f32[128]{0:T(128)S(1)} %get-tuple-element.9, f32[512,512]{1,0:T(8,128)} %get-tuple-element.13), kind=kOutput, calls=%fused_computation.98 | convolution fusion | flops 1611661312 | bytes 7602688 | tf_op jit(solution)/shard_map/dot_general | solution.py:21
  162.7 4.6 fusion.69
  171.1 3.8 fusion.63
  178.8 3.6 fusion.57
  182.5 4.0 fusion.54
  186.7 3.6 fusion.51
  190.4 3.6 fusion.48
  194.2 3.8 fusion.45
  201.8 3.6 fusion.39
  205.6 8.0 %fusion.100 = f32[512,512]{1,0:T(8,128)} fusion(f32[2048,512]{1,0:T(8,128)S(1)} %constant_dynamic-update-slice_fusion.12), kind=kOutput, calls=%fused_computation.157 | convolution fusion | flops 6442450944 | bytes 5242880 | tf_op jit(solution)/shard_map/dot_general | solution.py:35
  213.6 28.7 %convolution_bitcast_fusion = f32[2048,512]{1,0:T(8,128)} fusion(f32[2048,512]{1,0:T(8,128)S(1)} %constant_dynamic-update-slice_fusion.12, f32[2048,2048]{1,0:T(8,128)S(1)} %bitcast.55), kind=kOutput, calls=%fused_computation | convolution fusion | flops 25769803776 | bytes 25165824 | tf_op jit(solution)/shard_map/dot_general | solution.py:35
  242.3 184.7 %all-reduce.5.cloned.1.call-done = (f32[2048,512]{1,0:T(8,128)}, f32[512,512]{1,0:T(8,128)}) async-done(((f32[2048,512]{1,0:T(8,128)}, f32[512,512]{1,0:T(8,128)}), (f32[2048,512]{1,0:T(8,128)}, f32[512,512]{1,0:T(8,128)})) %all-reduce.5.cloned.1.call-update) | async-done | bytes 5242896 | tf_op jit(solution)/shard_map/psum | solution.py:53
  428.2 6.7 %fusion.36 = f32[2048,128]{1,0:T(8,128)S(1)} fusion(f32[2048,512]{1,0:T(8,128)} %copy-done, f32[2048,512]{1,0:T(8,128)} %get-tuple-element.10, f32[128]{0:T(128)S(1)} %get-tuple-element.5, f32[512,512]{1,0:T(8,128)} %get-tuple-element.11), kind=kOutput, calls=%fused_computation.49 | convolution fusion | flops 1611661312 | bytes 7602688 | tf_op jit(solution)/shard_map/dot_general | solution.py:21
  435.1 4.6 fusion.32
  443.6 3.8 fusion.26
  451.3 3.6 fusion.20
  455.0 4.0 fusion.17
  459.1 3.6 fusion.14
  466.6 3.8 fusion.8
  470.5 3.6 fusion.5
  474.3 3.6 fusion.2
  (69 shorter events, 35.4 us)
Async XLA Ops:
  7.2 147.4 %all-reduce.7.cloned.1.call-start = ((), (), s32[]{:S(2)}) async-start(), calls=%async_computation.1 | async-start | bytes 10485760 | tf_op jit(solution)/shard_map/psum | solution.py:49
  7.2 3.5 copy-start.9
  10.7 10.0 %copy-start = (f32[2048,512]{1,0:T(8,128)}, f32[2048,512]{1,0:T(8,128)S(1)}, u32[]{:S(2)}) copy-start(f32[2048,512]{1,0:T(8,128)S(1)} %copy.42) | copy-start | bytes 12582916
  10.7 10.0 %copy-start.10 = (f32[2048,2048]{1,0:T(8,128)S(1)}, f32[2048,2048]{1,0:T(8,128)}, u32[]{:S(2)}) copy-start(f32[2048,2048]{1,0:T(8,128)} %param.3) | copy-start | bytes 50331652
  49.0 378.0 %all-reduce.5.cloned.1.call-start = ((), (), s32[]{:S(2)}) async-start(), calls=%async_computation | async-start | bytes 10485760 | tf_op jit(solution)/shard_map/psum | solution.py:53
  154.6 7.9 %copy-start.3 = (f32[2048,512]{1,0:T(8,128)S(1)}, f32[2048,512]{1,0:T(8,128)}, u32[]{:S(2)}) copy-start(f32[2048,512]{1,0:T(8,128)} %copy.41) | copy-start | bytes 12582916
  155.8 6.8 %copy-start.5 = (f32[2048,512]{1,0:T(8,128)S(1)}, f32[2048,512]{1,0:T(8,128)}, u32[]{:S(2)}) copy-start(f32[2048,512]{1,0:T(8,128)} %get-tuple-element.12) | copy-start | bytes 12582916
  162.7 4.8 copy-start.7
  194.2 19.4 %slice-start = ((s8[16777216]{0:T(1024)(128)(4,1)}), s8[4194304]{0:T(1024)(128)(4,1)S(1)}, s32[]{:S(2)}) async-start(s8[16777216]{0:T(1024)(128)(4,1)} %bitcast.54), calls=%async_computation.2 | async-start | bytes 8388608
  198.1 15.5 %slice-start.1 = ((s8[16777216]{0:T(1024)(128)(4,1)}), s8[4194304]{0:T(1024)(128)(4,1)S(1)}, s32[]{:S(2)}) async-start(s8[16777216]{0:T(1024)(128)(4,1)} %bitcast.54), calls=%async_computation.3 | async-start | bytes 8388608
  201.8 11.8 %slice-start.2 = ((s8[16777216]{0:T(1024)(128)(4,1)}), s8[4194304]{0:T(1024)(128)(4,1)S(1)}, s32[]{:S(2)}) async-start(s8[16777216]{0:T(1024)(128)(4,1)} %bitcast.54), calls=%async_computation.4 | async-start | bytes 8388608
  205.6 8.0 %copy-start.4 = (f32[2048,512]{1,0:T(8,128)}, f32[2048,512]{1,0:T(8,128)S(1)}, u32[]{:S(2)}) copy-start(f32[2048,512]{1,0:T(8,128)S(1)} %constant_dynamic-update-slice_fusion.12) | copy-start | bytes 12582916
  205.6 8.0 %slice-start.3 = ((s8[16777216]{0:T(1024)(128)(4,1)}), s8[4194304]{0:T(1024)(128)(4,1)S(1)}, s32[]{:S(2)}) async-start(s8[16777216]{0:T(1024)(128)(4,1)} %bitcast.54), calls=%async_computation.5 | async-start | bytes 8388608
  427.0 7.9 %copy-start.1 = (f32[2048,512]{1,0:T(8,128)S(1)}, f32[2048,512]{1,0:T(8,128)}, u32[]{:S(2)}) copy-start(f32[2048,512]{1,0:T(8,128)} %copy-done) | copy-start | bytes 12582916
  428.2 6.8 %copy-start.6 = (f32[2048,512]{1,0:T(8,128)S(1)}, f32[2048,512]{1,0:T(8,128)}, u32[]{:S(2)}) copy-start(f32[2048,512]{1,0:T(8,128)} %get-tuple-element.10) | copy-start | bytes 12582916
  435.1 4.8 copy-start.8
  478.0 2.0 copy-start.2
Sparse Core Ops, SparseCore 0:
  49.1 105.3 all-reduce.6
  242.4 184.5 all-reduce.4
where the time goes:
time: 493 us; the launch traced here: 487 us
  waiting for transfers between devices  290 us (59%)
  matrix products  169 us (34%)
  between operations  14.7 us (3%)
  local copies, waits for them, and re-layouts  10.8 us (2%)
    psum x1, waiting for transfers between devices, shards(): prod_h, gram_w = lax.psum((prod_local_h, gram_w_local), 'samp')  185 us
    psum x1, waiting for transfers between devices, shards(): prod_w, gram_h = lax.psum((prod_local, gram_h_local), 'col')  105 us
    dot_general x24, matrix products, sweep_factor(): jnp.dot(factor, gram_cols, precision=lax.Precision.HIGHEST, preferred_ele...  95.8 us
    dot_general x3, matrix products, contract_rows(): lax.dot_general(left, right, (((0,), (0,)), ((), ())), precision=lax.Prec...  44.7 us
    dot_general x1, matrix products, shards(): jnp.dot(spectra, h_start, precision=lax.Precision.HIGHEST, preferred_elem...  28.3 us
  transfers between devices with their start and end apart: 2, of which 2 were waited for; matrix products, arithmetic and copies ran while one was open for 0% of the time, Pallas kernels for 0%

commit v1 on v0

v1 whole, which is shorter than its diff:
```python
import functools

import jax
import jax.numpy as jnp
from jax import lax
from jax.experimental import pallas as pl
from jax.experimental.pallas import tpu as pltpu
from jax.sharding import PartitionSpec as P

BLOCK = 128
SWEEPS = 3
FLOOR = 1e-06
MESH = pl.DeviceIdType.MESH
F32 = jnp.float32
BF16 = jnp.bfloat16
CORES = 2
DEPTH = 4
PIECES = 4
TILE = 256


def split(x):
    high = x.astype(BF16)
    return high, (x - high.astype(F32)).astype(BF16)


def dot(a, b):
    return jnp.dot(a, b, preferred_element_type=F32)


def dot3(ah, al, bh, bl):
    return dot(ah, bh) + (dot(ah, bl) + dot(al, bh))


def kernel(
    n_samp, n_col, spectra, w_start, h_start, w_out, h_out,
    spec, w_full, h_full, hh, hl, wth, wtl, pt, prod, acc, xrecv, ring_a, ring_b,
    gp, gcore, gring_a, gring_b, gx, gram, gcat, fh, fl,
    load_sem, core_sem, x_sem, ag_sem, fwd_sem, ring_sem, back_sem,
    gcore_sem, gring_sem, gx_sem, gback_sem, gout_sem, out_sem,
):
    rows, rank = w_full.shape
    cols = h_full.shape[0]
    chips = n_col // CORES
    rb = rows // n_col
    qb = cols // n_samp
    half_rank = rank // 2
    gb = half_rank // n_samp

    samp = lax.axis_index("samp")
    col = lax.axis_index("col")
    core = lax.rem(col, CORES)
    chip = col // CORES
    mate = {"col": chip * CORES + 1 - core}
    x_right = {"col": lax.rem(chip + 1, chips) * CORES + core}
    x_left = {"col": lax.rem(chip + chips - 1, chips) * CORES + core}
    width = n_samp // DEPTH
    z, y = samp // width, lax.rem(samp, width)
    pos = y * DEPTH + z + lax.rem(y, 2) * (DEPTH - 1 - 2 * z)

    def member(p):
        p = lax.rem(p + 2 * n_samp, n_samp)
        py, pr = p // DEPTH, lax.rem(p, DEPTH)
        pz = pr + lax.rem(py, 2) * (DEPTH - 1 - 2 * pr)
        return pz * width + py

    ring_next = {"samp": member(pos + 1)}
    ring_prev = {"samp": member(pos - 1)}

    def rows_at(start, size):
        return pl.ds(pl.multiple_of(start, size), size)

    def remote(src, dst, sems, index, device):
        return pltpu.make_async_remote_copy(
            src_ref=src, dst_ref=dst, send_sem=sems.at[(0,) + index], recv_sem=sems.at[(1,) + index],
            device_id=device, device_id_type=MESH,
        )

    sent = []

    def send(*args):
        copy = remote(*args)
        copy.start()
        sent.append(copy)
        return copy

    h_load = pltpu.make_async_copy(h_start, h_full, load_sem.at[0])
    h_load.start()
    order = []
    for t in range(chips):
        dest = lax.rem(chip - 1 - t + 2 * chips, chips)
        order.append((dest, dest * CORES + 1 - core, dest * CORES + core))
    spec_loads = []
    for t, (_, first, second) in enumerate(order):
        for u, blk in enumerate((first, second)):
            copy = pltpu.make_async_copy(
                spectra.at[rows_at(blk * rb, rb)], spec.at[rows_at(blk * rb, rb)], load_sem.at[2 + 2 * t + u]
            )
            copy.start()
            spec_loads.append(copy)
    own_w = rows_at(col * rb, rb)
    w_load = pltpu.make_async_copy(w_start.at[own_w], w_full.at[own_w], load_sem.at[1])
    w_load.start()

    barrier = pltpu.get_barrier_semaphore()
    greet = [mate, x_right, x_left, ring_next, ring_prev]
    for device in greet:
        pl.semaphore_signal(barrier, inc=1, device_id=device, device_id_type=MESH)
    pl.semaphore_wait(barrier, len(greet))

    def ring_reduce(data, base, block, recv_a, recv_b, sems):
        part = block // 2
        last = None
        for t in range(n_samp):
            current = []
            for way, (recv, device, sign) in enumerate(((recv_a, ring_next, 1), (recv_b, ring_prev, -1))):
                owner = member(pos - sign * (1 + t))
                where = rows_at(base + owner * block + way * part, part)
                if t > 0:
                    last[way].wait_recv()
                    data[where] += recv[t - 1]
                if t < n_samp - 1:
                    current.append(send(data.at[where], recv.at[t], sems, (way, t), device))
            last = current
            yield

    def ring_gather(data, base, block, sems):
        part = block // 2
        last = None
        for t in range(n_samp):
            current = []
            for way, (device, sign) in enumerate(((ring_next, 1), (ring_prev, -1))):
                owner = member(pos - sign * t)
                where = rows_at(base + owner * block + way * part, part)
                if t > 0:
                    last[way].wait_recv()
                if t < n_samp - 1:
                    current.append(send(data.at[where], data.at[where], sems, (way, t), device))
            last = current
            yield

    def gram_sum(i):
        mine = core * half_rank
        other = (1 - core) * half_rank
        copy = send(gp.at[i, rows_at(other, half_rank)], gcore.at[i], gcore_sem, (i,), mate)
        yield
        copy.wait_recv()
        gp[i, rows_at(mine, half_rank)] += gcore[i]
        yield from ring_reduce(gp.at[i], mine, gb, gring_a.at[i], gring_b.at[i], gring_sem.at[:, i])
        own = rows_at(mine + samp * gb, gb)
        total = gp[i, own]
        for t in range(chips - 1):
            source = gp.at[i, own] if t == 0 else gx.at[i, t - 1]
            copy = send(source, gx.at[i, t], gx_sem, (i, t), x_right)
            yield
            copy.wait_recv()
            total = total + gx[i, t]
        gram[i, own] = total
        yield from ring_gather(gram.at[i], mine, gb, gback_sem.at[:, i])
        where = rows_at(mine, half_rank)
        copy = send(gram.at[i, where], gram.at[i, where], gout_sem, (i,), mate)
        yield
        copy.wait_recv()

    def sweep(factor, product, g):
        n = factor.shape[0]
        scale = []
        for b in range(rank // BLOCK):
            cols_b = slice(b * BLOCK, (b + 1) * BLOCK)
            high, low = split(gram[g, :, cols_b])
            gcat[b, :, :BLOCK] = high
            gcat[b, :, BLOCK:] = low
            scale.append(1.0 / jnp.sum(gram[g, cols_b, cols_b], axis=0, keepdims=True))
            high, low = split(factor[:, cols_b])
            fh[:n, cols_b] = high
            fl[:n, cols_b] = low

        def one(_, carry):
            for b in range(rank // BLOCK):
                cols_b = slice(b * BLOCK, (b + 1) * BLOCK)
                both = dot(fh[:n], gcat[b])
                low = dot(fl[:n], gcat[b, :, :BLOCK])
                fg = both[:, :BLOCK] + (both[:, BLOCK:] + low)
                block = jnp.maximum(factor[:, cols_b] + (product[:, cols_b] - fg) * scale[b], FLOOR)
                factor[:, cols_b] = block
                high, low = split(block)
                fh[:n, cols_b] = high
                fl[:n, cols_b] = low
            return carry

        lax.fori_loop(0, SWEEPS, one, 0)

    h_load.wait()
    share = h_full[rows_at(samp * qb, qb)]
    th, tl = split(share.T)
    bh, bl = split(share)
    gp[0] = dot3(th, tl, bh, bl)
    gram_h = gram_sum(0)
    next(gram_h)

    def split_h(i, carry):
        where = rows_at(i * TILE, TILE)
        hh[where], hl[where] = split(h_full[where])
        return carry

    lax.fori_loop(0, cols // TILE, split_h, 0)

    def product_block(blk, store):
        tile = min(TILE, rb)

        def body(i, carry):
            sh, sl = split(spec[rows_at(blk * rb + i * tile, tile)])
            store[rows_at(i * tile, tile)] = dot3(sh, sl, hh[...], hl[...])
            return carry

        lax.fori_loop(0, rb // tile, body, 0)

    x_copy = None
    for t, (_, first, second) in enumerate(order):
        outgoing = prod.at[pl.ds(t * rb, rb)]
        incoming = prod.at[pl.ds((chips + t) * rb, rb)]
        spec_loads[2 * t].wait()
        product_block(first, outgoing)
        core_copy = send(outgoing, incoming, core_sem, (t,), mate)
        next(gram_h)
        spec_loads[2 * t + 1].wait()
        product_block(second, acc.at[t])
        core_copy.wait_recv()
        acc[t] += incoming[...]
        if t < chips - 1:
            if t > 0:
                x_copy.wait_recv()
                acc[t] += xrecv[t - 1]
            x_copy = send(acc.at[t], xrecv.at[t], x_sem, (t,), x_right)
        next(gram_h)
    for _ in gram_h:
        pass
    x_copy.wait_recv()
    acc[chips - 1] += xrecv[chips - 2]

    w_load.wait()
    sweep(w_full.at[own_w], acc.at[chips - 1], 0)

    for copy in sent:
        copy.wait_send()
    sent.clear()
    piece = rb // PIECES

    def w_piece(block, q):
        return w_full.at[rows_at(block * rb + q * piece, piece)]

    x_arrivals = [send(w_piece(col, q), w_piece(col, q), ag_sem, (0, q), x_right) for q in range(PIECES)]
    mate_arrivals = [send(w_piece(col, q), w_piece(col, q), fwd_sem, (0, q), mate) for q in range(PIECES)]

    def transpose_into(t, block, half):
        step = min(TILE, rb)
        for i in range(rb // step):
            high, low = split(w_full[rows_at(block * rb + i * step, step)].T)
            where = rows_at(half * rb + i * step, step)
            wth[t, :, where] = high
            wtl[t, :, where] = low

    transpose_into(0, col, core)
    lanes = rows_at(core * rb, rb)
    bh, bl = split(w_full[own_w])
    gp[1] = dot3(wth[0, :, lanes], wtl[0, :, lanes], bh, bl)
    gram_w = gram_sum(1)
    next(gram_w)
    for copy in mate_arrivals:
        copy.wait_recv()
    transpose_into(0, chip * CORES + 1 - core, 1 - core)
    next(gram_w)

    def product_tiles(t, source):
        span = CORES * rb

        def body(i, carry):
            lane = rows_at(i * TILE, TILE)
            sh, sl = split(spec[rows_at(source * span, span), lane])
            part = dot3(wth[t], wtl[t], sh, sl)
            if t > 0:
                part = part + pt[:, lane]
            if t == chips - 1:
                prod[lane] = part.T
            else:
                pt[:, lane] = part
            return carry

        lax.fori_loop(0, cols // TILE, body, 0)

    product_tiles(0, chip)
    for t in range(1, chips):
        source = lax.rem(chip - t + chips, chips)
        same = source * CORES + core
        later, mate_copies = [], []
        for q in range(PIECES):
            x_arrivals[q].wait_recv()
            if t < chips - 1:
                later.append(send(w_piece(same, q), w_piece(same, q), ag_sem, (t, q), x_right))
            mate_copies.append(send(w_piece(same, q), w_piece(same, q), fwd_sem, (t, q), mate))
            next(gram_w)
        x_arrivals = later
        transpose_into(t, same, core)
        for copy in mate_copies:
            copy.wait_recv()
        transpose_into(t, source * CORES + 1 - core, 1 - core)
        product_tiles(t, source)
    w_store = pltpu.make_async_copy(w_full, w_out, out_sem.at[0])
    w_store.start()

    for _ in ring_reduce(prod, 0, qb, ring_a, ring_b, ring_sem):
        next(gram_w, None)
    for _ in gram_w:
        pass

    own_h = rows_at(samp * qb, qb)
    sweep(h_full.at[own_h], prod.at[own_h], 1)
    for _ in ring_gather(h_full, 0, qb, back_sem):
        pass
    h_store = pltpu.make_async_copy(h_full, h_out, out_sem.at[1])
    h_store.start()
    for copy in sent:
        copy.wait_send()
    w_store.wait()
    h_store.wait()


def shards(n_samp, n_col, spectra, w_start, h_start):
    rows, rank = w_start.shape
    cols = h_start.shape[0]
    chips = n_col // CORES
    rb, qb, gb = rows // n_col, cols // n_samp, rank // 2 // n_samp
    dma = pltpu.SemaphoreType.DMA
    hops = n_samp - 1
    scratch = [
        pltpu.VMEM((rows, cols), F32),
        pltpu.VMEM((rows, rank), F32),
        pltpu.VMEM((cols, rank), F32),
        pltpu.VMEM((cols, rank), BF16),
        pltpu.VMEM((cols, rank), BF16),
        pltpu.VMEM((chips, rank, CORES * rb), BF16),
        pltpu.VMEM((chips, rank, CORES * rb), BF16),
        pltpu.VMEM((rank, cols), F32),
        pltpu.VMEM((max(rows, cols), rank), F32),
        pltpu.VMEM((chips, rb, rank), F32),
        pltpu.VMEM((chips - 1, rb, rank), F32),
        pltpu.VMEM((hops, qb // 2, rank), F32),
        pltpu.VMEM((hops, qb // 2, rank), F32),
        pltpu.VMEM((2, rank, rank), F32),
        pltpu.VMEM((2, rank // 2, rank), F32),
        pltpu.VMEM((2, hops, gb // 2, rank), F32),
        pltpu.VMEM((2, hops, gb // 2, rank), F32),
        pltpu.VMEM((2, chips - 1, gb, rank), F32),
        pltpu.VMEM((2, rank, rank), F32),
        pltpu.VMEM((rank // BLOCK, rank, 2 * BLOCK), BF16),
        pltpu.VMEM((max(rb, qb), rank), BF16),
        pltpu.VMEM((max(rb, qb), rank), BF16),
        dma((2 + 2 * chips,)),
        dma((2, chips)),
        dma((2, chips)),
        dma((2, chips, PIECES)),
        dma((2, chips, PIECES)),
        dma((2, 2, n_samp)),
        dma((2, 2, n_samp)),
        dma((2, 2)),
        dma((2, 2, 2, n_samp)),
        dma((2, 2, chips)),
        dma((2, 2, 2, n_samp)),
        dma((2, 2)),
        dma((2,)),
    ]
    return pl.pallas_call(
        functools.partial(kernel, n_samp, n_col),
        out_shape=(
            jax.ShapeDtypeStruct((rows, rank), F32),
            jax.ShapeDtypeStruct((cols, rank), F32),
        ),
        in_specs=[pl.BlockSpec(memory_space=pl.ANY)] * 3,
        out_specs=[pl.BlockSpec(memory_space=pl.ANY)] * 2,
        scratch_shapes=scratch,
        compiler_params=pltpu.CompilerParams(
            collective_id=0, has_side_effects=True, vmem_limit_bytes=63 * 1024 * 1024
        ),
    )(spectra, w_start, h_start)


def solution(mesh):
    return jax.shard_map(
        functools.partial(shards, mesh.shape["samp"], mesh.shape["col"]),
        mesh=mesh,
        in_specs=(P("samp", "col"), P("samp", None), P("col", None)),
        out_specs=(P("samp", None), P("col", None)),
        check_vma=False,
    )
```

time: 493 us -> 224 us (0.45); the launches traced: 487 us -> 224 us
  waiting for transfers between devices: 290 us -> 0 us
  Pallas kernels: 0 us -> 217 us
  matrix products: 169 us -> 0 us
  between operations: 14.7 us -> 0.65 us
    psum x2 -> x0, waiting for transfers between devices: 290 us -> none  [the longest x1 185 us: shards(): prod_h, gram_w = lax.psum((prod_local_h, gram_w_local), 'samp')]
    pallas_call x0 -> x1, Pallas kernels: none -> 217 us  [shards(): pl.pallas_call(functools.partial(kernel, n_samp, n_col), out_shape=(jax.S...]
    dot_general x28 -> x0, matrix products: 169 us -> none  [the longest x24 95.8 us: sweep_factor(): jnp.dot(factor, gram_cols, precision=lax.Precision.HIGHEST, preferred_ele...]
  transfers between devices with their start and end apart: 2 -> 0, of which waited for: 2 -> 0; matrix products, arithmetic and copies ran while one was open for 0% -> 0% of each run, Pallas kernels for 0% -> 0%
where the time goes in v1:
time: 224 us
  Pallas kernels  217 us (97%)
  local copies, waits for them, and re-layouts  6.84 us (3%)
    pallas_call x1, Pallas kernels, shards(): pl.pallas_call(functools.partial(kernel, n_samp, n_col), out_shape=(jax.S...  217 us
    unnamed x4, local copies, waits for them, and re-layouts  6.84 us

profile of v1, /device:TPU:0, one launch (start us, length us, event | category | flops | bytes accessed | tf_op | source)
XLA Modules:
  0.0 224.3 jit_solution(14876892097511112139)
XLA Ops:
  0.6 216.8 %shard_map.50 = (f32[2048,512]{1,0:T(8,128)}, f32[2048,512]{1,0:T(8,128)}) custom-call(f32[2048,2048]{1,0:T(8,128)} %spectra.1, f32[2048,512]{1,0:T(8,128)} %w_start.1, f32[2048,512]{1,0:T(8,128)} %h_start.1), custom_call_target="tpu_custom_call" | custom-call | tf_op jit(solution)/shard_map/pallas_call | solution.py:372
  217.5 0.0 copy-start
  217.5 4.8 %copy.7 = f32[2048,512]{1,0:T(8,128)} copy(f32[2048,512]{1,0:T(8,128)} %get-tuple-element.4) | data formatting | bytes 8388608
  222.3 0.0 copy-done
  222.3 2.0 copy.8
Async XLA Ops:
  217.5 4.8 %copy-start = (f32[2048,512]{1,0:T(8,128)S(1)}, f32[2048,512]{1,0:T(8,128)}, u32[]{:S(2)}) copy-start(f32[2048,512]{1,0:T(8,128)} %get-tuple-element.5) | copy-start | bytes 12582916

commit v2 on v1

--- a/solution.py
+++ b/solution.py
@@ -16,6 +16,8 @@
 CORES = 2
 DEPTH = 4
 PIECES = 4
+HALVES = 2
+CHAINS = 4
 TILE = 256
 
 
@@ -35,7 +37,7 @@
 def kernel(
     n_samp, n_col, spectra, w_start, h_start, w_out, h_out,
     spec, w_full, h_full, hh, hl, wth, wtl, pt, prod, acc, xrecv, ring_a, ring_b,
-    gp, gcore, gring_a, gring_b, gx, gram, gcat, fh, fl,
+    gp, gcore, gring, gx, gram, gcat, fh, fl,
     load_sem, core_sem, x_sem, ag_sem, fwd_sem, ring_sem, back_sem,
     gcore_sem, gring_sem, gx_sem, gback_sem, gout_sem, out_sem,
 ):
@@ -103,41 +105,44 @@
     w_load.start()
 
     barrier = pltpu.get_barrier_semaphore()
-    greet = [mate, x_right, x_left, ring_next, ring_prev]
+    greet = [mate, x_right, x_left]
+    greet += [{"samp": lax.rem(samp + o, n_samp)} for o in range(1, n_samp)]
     for device in greet:
         pl.semaphore_signal(barrier, inc=1, device_id=device, device_id_type=MESH)
     pl.semaphore_wait(barrier, len(greet))
 
-    def ring_reduce(data, base, block, recv_a, recv_b, sems):
-        part = block // 2
-        last = None
+    part = qb // 2 // CHAINS
+    lines = [(way, q) for q in range(CHAINS) for way in (0, 1)]
+
+    def ring_rows(sign, away, way, q):
+        owner = member(pos - sign * away)
+        return rows_at(owner * qb + (way * CHAINS + q) * part, part)
+
+    def ring_reduce(data, prepare):
+        last = {}
         for t in range(n_samp):
-            current = []
-            for way, (recv, device, sign) in enumerate(((recv_a, ring_next, 1), (recv_b, ring_prev, -1))):
-                owner = member(pos - sign * (1 + t))
-                where = rows_at(base + owner * block + way * part, part)
+            prepare(t)
+            for way, q in lines:
+                recv, device, sign = ((ring_a, ring_next, 1), (ring_b, ring_prev, -1))[way]
+                where = ring_rows(sign, 1 + t, way, q)
                 if t > 0:
-                    last[way].wait_recv()
-                    data[where] += recv[t - 1]
+                    last[way, q].wait_recv()
+                    data[where] += recv[t - 1, q * part : (q + 1) * part]
                 if t < n_samp - 1:
-                    current.append(send(data.at[where], recv.at[t], sems, (way, t), device))
-            last = current
+                    slot = recv.at[t, pl.ds(q * part, part)]
+                    last[way, q] = send(data.at[where], slot, ring_sem, (way, t, q), device)
             yield
 
-    def ring_gather(data, base, block, sems):
-        part = block // 2
-        last = None
+    def ring_gather(data):
+        last = {}
         for t in range(n_samp):
-            current = []
-            for way, (device, sign) in enumerate(((ring_next, 1), (ring_prev, -1))):
-                owner = member(pos - sign * t)
-                where = rows_at(base + owner * block + way * part, part)
+            for way, q in lines:
+                device, sign = ((ring_next, 1), (ring_prev, -1))[way]
+                where = ring_rows(sign, t, way, q)
                 if t > 0:
-                    last[way].wait_recv()
+                    last[way, q].wait_recv()
                 if t < n_samp - 1:
-                    current.append(send(data.at[where], data.at[where], sems, (way, t), device))
-            last = current
-            yield
+                    last[way, q] = send(data.at[where], data.at[where], back_sem, (way, t, q), device)
 
     def gram_sum(i):
         mine = core * half_rank
@@ -146,9 +151,18 @@
         yield
         copy.wait_recv()
         gp[i, rows_at(mine, half_rank)] += gcore[i]
-        yield from ring_reduce(gp.at[i], mine, gb, gring_a.at[i], gring_b.at[i], gring_sem.at[:, i])
+        copies = []
+        for o in range(1, n_samp):
+            peer = lax.rem(samp + o, n_samp)
+            block = gp.at[i, rows_at(mine + peer * gb, gb)]
+            copies.append(send(block, gring.at[i, o - 1], gring_sem, (i, o - 1), {"samp": peer}))
+        yield
         own = rows_at(mine + samp * gb, gb)
         total = gp[i, own]
+        for o in range(1, n_samp):
+            copies[o - 1].wait_recv()
+            total = total + gring[i, o - 1]
+        gp[i, own] = total
         for t in range(chips - 1):
             source = gp.at[i, own] if t == 0 else gx.at[i, t - 1]
             copy = send(source, gx.at[i, t], gx_sem, (i, t), x_right)
@@ -156,14 +170,19 @@
             copy.wait_recv()
             total = total + gx[i, t]
         gram[i, own] = total
-        yield from ring_gather(gram.at[i], mine, gb, gback_sem.at[:, i])
+        copies = []
+        for o in range(1, n_samp):
+            peer = lax.rem(samp + o, n_samp)
+            copies.append(send(gram.at[i, own], gram.at[i, own], gback_sem, (i, o - 1), {"samp": peer}))
+        yield
+        for copy in copies:
+            copy.wait_recv()
         where = rows_at(mine, half_rank)
         copy = send(gram.at[i, where], gram.at[i, where], gout_sem, (i,), mate)
         yield
         copy.wait_recv()
 
-    def sweep(factor, product, g):
-        n = factor.shape[0]
+    def sweep_scale(g):
         scale = []
         for b in range(rank // BLOCK):
             cols_b = slice(b * BLOCK, (b + 1) * BLOCK)
@@ -171,6 +190,12 @@
             gcat[b, :, :BLOCK] = high
             gcat[b, :, BLOCK:] = low
             scale.append(1.0 / jnp.sum(gram[g, cols_b, cols_b], axis=0, keepdims=True))
+        return scale
+
+    def sweep(factor, product, scale):
+        n = factor.shape[0]
+        for b in range(rank // BLOCK):
+            cols_b = slice(b * BLOCK, (b + 1) * BLOCK)
             high, low = split(factor[:, cols_b])
             fh[:n, cols_b] = high
             fl[:n, cols_b] = low
@@ -205,52 +230,55 @@
 
     lax.fori_loop(0, cols // TILE, split_h, 0)
 
-    def product_block(blk, store):
-        tile = min(TILE, rb)
-
-        def body(i, carry):
-            sh, sl = split(spec[rows_at(blk * rb + i * tile, tile)])
-            store[rows_at(i * tile, tile)] = dot3(sh, sl, hh[...], hl[...])
-            return carry
-
-        lax.fori_loop(0, rb // tile, body, 0)
-
-    x_copy = None
+    tile = rb // HALVES
+
+    def product_rows(blk, u):
+        sh, sl = split(spec[rows_at(blk * rb + u * tile, tile)])
+        return dot3(sh, sl, hh[...], hl[...])
+
+    x_copies = {}
     for t, (_, first, second) in enumerate(order):
-        outgoing = prod.at[pl.ds(t * rb, rb)]
-        incoming = prod.at[pl.ds((chips + t) * rb, rb)]
-        spec_loads[2 * t].wait()
-        product_block(first, outgoing)
-        core_copy = send(outgoing, incoming, core_sem, (t,), mate)
-        next(gram_h)
-        spec_loads[2 * t + 1].wait()
-        product_block(second, acc.at[t])
-        core_copy.wait_recv()
-        acc[t] += incoming[...]
-        if t < chips - 1:
-            if t > 0:
-                x_copy.wait_recv()
-                acc[t] += xrecv[t - 1]
-            x_copy = send(acc.at[t], xrecv.at[t], x_sem, (t,), x_right)
-        next(gram_h)
+        for u in range(HALVES):
+            piece_rows = pl.ds(u * tile, tile)
+            outgoing = prod.at[pl.ds(t * rb + u * tile, tile)]
+            incoming = prod.at[pl.ds((chips + t) * rb + u * tile, tile)]
+            if u == 0:
+                spec_loads[2 * t].wait()
+            outgoing[...] = product_rows(first, u)
+            core_copy = send(outgoing, incoming, core_sem, (t, u), mate)
+            if u == 0:
+                spec_loads[2 * t + 1].wait()
+            acc[t, piece_rows] = product_rows(second, u)
+            core_copy.wait_recv()
+            acc[t, piece_rows] += incoming[...]
+            if t < chips - 1:
+                if t > 0:
+                    x_copies[t - 1, u].wait_recv()
+                    acc[t, piece_rows] += xrecv[t - 1, piece_rows]
+                x_copies[t, u] = send(acc.at[t, piece_rows], xrecv.at[t, piece_rows], x_sem, (t, u), x_right)
+            next(gram_h, None)
     for _ in gram_h:
         pass
-    x_copy.wait_recv()
-    acc[chips - 1] += xrecv[chips - 2]
-
-    w_load.wait()
-    sweep(w_full.at[own_w], acc.at[chips - 1], 0)
-
-    for copy in sent:
-        copy.wait_send()
+    early = list(sent)
     sent.clear()
+
     piece = rb // PIECES
+    each = PIECES // HALVES
 
     def w_piece(block, q):
         return w_full.at[rows_at(block * rb + q * piece, piece)]
 
-    x_arrivals = [send(w_piece(col, q), w_piece(col, q), ag_sem, (0, q), x_right) for q in range(PIECES)]
-    mate_arrivals = [send(w_piece(col, q), w_piece(col, q), fwd_sem, (0, q), mate) for q in range(PIECES)]
+    w_load.wait()
+    scale = sweep_scale(0)
+    x_arrivals, mate_arrivals = [], []
+    for u in range(HALVES):
+        piece_rows = pl.ds(u * tile, tile)
+        x_copies[chips - 2, u].wait_recv()
+        acc[chips - 1, piece_rows] += xrecv[chips - 2, piece_rows]
+        sweep(w_full.at[rows_at(col * rb + u * tile, tile)], acc.at[chips - 1, piece_rows], scale)
+        for q in range(u * each, (u + 1) * each):
+            x_arrivals.append(send(w_piece(col, q), w_piece(col, q), ag_sem, (0, q), x_right))
+            mate_arrivals.append(send(w_piece(col, q), w_piece(col, q), fwd_sem, (0, q), mate))
 
     def transpose_into(t, block, half):
         step = min(TILE, rb)
@@ -271,23 +299,27 @@
     transpose_into(0, chip * CORES + 1 - core, 1 - core)
     next(gram_w)
 
+    def product_tile(t, source, start, size):
+        span = CORES * rb
+        lane = rows_at(start, size)
+        sh, sl = split(spec[rows_at(source * span, span), lane])
+        partial = dot3(wth[t], wtl[t], sh, sl)
+        if t > 0:
+            partial = partial + pt[:, lane]
+        if t == chips - 1:
+            prod[lane] = partial.T
+        else:
+            pt[:, lane] = partial
+
     def product_tiles(t, source):
-        span = CORES * rb
-
         def body(i, carry):
-            lane = rows_at(i * TILE, TILE)
-            sh, sl = split(spec[rows_at(source * span, span), lane])
-            part = dot3(wth[t], wtl[t], sh, sl)
-            if t > 0:
-                part = part + pt[:, lane]
-            if t == chips - 1:
-                prod[lane] = part.T
-            else:
-                pt[:, lane] = part
+            product_tile(t, source, i * TILE, TILE)
             return carry
 
         lax.fori_loop(0, cols // TILE, body, 0)
 
+    for copy in early:
+        copy.wait_send()
     product_tiles(0, chip)
     for t in range(1, chips):
         source = lax.rem(chip - t + chips, chips)
@@ -298,25 +330,43 @@
             if t < chips - 1:
                 later.append(send(w_piece(same, q), w_piece(same, q), ag_sem, (t, q), x_right))
             mate_copies.append(send(w_piece(same, q), w_piece(same, q), fwd_sem, (t, q), mate))
-            next(gram_w)
+            next(gram_w, None)
         x_arrivals = later
         transpose_into(t, same, core)
         for copy in mate_copies:
             copy.wait_recv()
         transpose_into(t, source * CORES + 1 - core, 1 - core)
-        product_tiles(t, source)
+        if t < chips - 1 or qb % BLOCK:
+            product_tiles(t, source)
     w_store = pltpu.make_async_copy(w_full, w_out, out_sem.at[0])
     w_store.start()
 
-    for _ in ring_reduce(prod, 0, qb, ring_a, ring_b, ring_sem):
-        next(gram_w, None)
+    source = lax.rem(chip + 1, chips)
+
+    def prepare(t):
+        if qb % BLOCK:
+            return
+
+        def body(i, carry):
+            product_tile(chips - 1, source, member(pos + (1 - 2 * i) * (1 + t)) * qb, qb)
+            return carry
+
+        if t < n_samp // 2 - 1:
+            lax.fori_loop(0, 2, body, 0)
+        elif t == n_samp // 2 - 1:
+            product_tile(chips - 1, source, member(pos + n_samp // 2) * qb, qb)
+        elif t == n_samp // 2:
+            product_tile(chips - 1, source, samp * qb, qb)
+
+    for t, _ in enumerate(ring_reduce(prod, prepare)):
+        if t >= n_samp // 2:
+            next(gram_w, None)
     for _ in gram_w:
         pass
 
     own_h = rows_at(samp * qb, qb)
-    sweep(h_full.at[own_h], prod.at[own_h], 1)
-    for _ in ring_gather(h_full, 0, qb, back_sem):
-        pass
+    sweep(h_full.at[own_h], prod.at[own_h], sweep_scale(1))
+    ring_gather(h_full)
     h_store = pltpu.make_async_copy(h_full, h_out, out_sem.at[1])
     h_store.start()
     for copy in sent:
@@ -348,24 +398,23 @@
         pltpu.VMEM((hops, qb // 2, rank), F32),
         pltpu.VMEM((2, rank, rank), F32),
         pltpu.VMEM((2, rank // 2, rank), F32),
-        pltpu.VMEM((2, hops, gb // 2, rank), F32),
-        pltpu.VMEM((2, hops, gb // 2, rank), F32),
+        pltpu.VMEM((2, hops, gb, rank), F32),
         pltpu.VMEM((2, chips - 1, gb, rank), F32),
         pltpu.VMEM((2, rank, rank), F32),
         pltpu.VMEM((rank // BLOCK, rank, 2 * BLOCK), BF16),
         pltpu.VMEM((max(rb, qb), rank), BF16),
         pltpu.VMEM((max(rb, qb), rank), BF16),
         dma((2 + 2 * chips,)),
-        dma((2, chips)),
-        dma((2, chips)),
+        dma((2, chips, HALVES)),
+        dma((2, chips, HALVES)),
         dma((2, chips, PIECES)),
         dma((2, chips, PIECES)),
+        dma((2, 2, n_samp, CHAINS)),
+        dma((2, 2, n_samp, CHAINS)),
+        dma((2, 2)),
         dma((2, 2, n_samp)),
+        dma((2, 2, chips)),
         dma((2, 2, n_samp)),
-        dma((2, 2)),
-        dma((2, 2, 2, n_samp)),
-        dma((2, 2, chips)),
-        dma((2, 2, 2, n_samp)),
         dma((2, 2)),
         dma((2,)),
     ]

time: 224 us -> 195 us (0.87)
  Pallas kernels: 217 us -> 187 us
    pallas_call x1, Pallas kernels: 217 us -> 187 us  [shards(): pl.pallas_call(functools.partial(kernel, n_samp, n_col), out_shape=(jax.S...]
where the time goes in v2:
time: 195 us; the launch traced here: 194 us
  Pallas kernels  187 us (96%)
  local copies, waits for them, and re-layouts  6.84 us (4%)
    pallas_call x1, Pallas kernels, shards(): pl.pallas_call(functools.partial(kernel, n_samp, n_col), out_shape=(jax.S...  187 us
    unnamed x4, local copies, waits for them, and re-layouts  6.84 us

profile of v2, /device:TPU:0, one launch (start us, length us, event | category | flops | bytes accessed | tf_op | source)
XLA Modules:
  0.0 194.5 jit_solution(11735384447402157330)
XLA Ops:
  0.6 187.0 %shard_map.50 = (f32[2048,512]{1,0:T(8,128)}, f32[2048,512]{1,0:T(8,128)}) custom-call(f32[2048,2048]{1,0:T(8,128)} %spectra.1, f32[2048,512]{1,0:T(8,128)} %w_start.1, f32[2048,512]{1,0:T(8,128)} %h_start.1), custom_call_target="tpu_custom_call" | custom-call | tf_op jit(solution)/shard_map/pallas_call | solution.py:421
  187.6 0.0 copy-start
  187.6 4.8 %copy.7 = f32[2048,512]{1,0:T(8,128)} copy(f32[2048,512]{1,0:T(8,128)} %get-tuple-element.4) | data formatting | bytes 8388608
  192.4 0.0 copy-done
  192.4 2.0 %copy.8 = f32[2048,512]{1,0:T(8,128)} copy(f32[2048,512]{1,0:T(8,128)S(1)} %copy-done) | data formatting | bytes 8388608
Async XLA Ops:
  187.6 4.8 %copy-start = (f32[2048,512]{1,0:T(8,128)S(1)}, f32[2048,512]{1,0:T(8,128)}, u32[]{:S(2)}) copy-start(f32[2048,512]{1,0:T(8,128)} %get-tuple-element.5) | copy-start | bytes 12582916

commit v3 on v2

--- a/solution.py
+++ b/solution.py
@@ -17,7 +17,7 @@
 DEPTH = 4
 PIECES = 4
 HALVES = 2
-CHAINS = 4
+CHAINS = 2
 TILE = 256
 
 

time: 195 us -> 194 us (level)
  no operation moved by 1% of the time
where the time goes in v3:
time: 194 us
  Pallas kernels  186 us (96%)
  local copies, waits for them, and re-layouts  6.84 us (4%)
    pallas_call x1, Pallas kernels, shards(): pl.pallas_call(functools.partial(kernel, n_samp, n_col), out_shape=(jax.S...  186 us
    unnamed x4, local copies, waits for them, and re-layouts  6.84 us

profile of v3, /device:TPU:0, one launch (start us, length us, event | category | flops | bytes accessed | tf_op | source)
XLA Modules:
  0.0 193.8 jit_solution(18353351624931093988)
XLA Ops:
  0.6 186.3 %shard_map.50 = (f32[2048,512]{1,0:T(8,128)}, f32[2048,512]{1,0:T(8,128)}) custom-call(f32[2048,2048]{1,0:T(8,128)} %spectra.1, f32[2048,512]{1,0:T(8,128)} %w_start.1, f32[2048,512]{1,0:T(8,128)} %h_start.1), custom_call_target="tpu_custom_call" | custom-call | tf_op jit(solution)/shard_map/pallas_call | solution.py:421
  186.9 0.0 copy-start
  187.0 4.8 %copy.7 = f32[2048,512]{1,0:T(8,128)} copy(f32[2048,512]{1,0:T(8,128)} %get-tuple-element.4) | data formatting | bytes 8388608
  191.8 0.0 copy-done
  191.8 2.0 %copy.8 = f32[2048,512]{1,0:T(8,128)} copy(f32[2048,512]{1,0:T(8,128)S(1)} %copy-done) | data formatting | bytes 8388608
Async XLA Ops:
  186.9 4.8 %copy-start = (f32[2048,512]{1,0:T(8,128)S(1)}, f32[2048,512]{1,0:T(8,128)}, u32[]{:S(2)}) copy-start(f32[2048,512]{1,0:T(8,128)} %get-tuple-element.5) | copy-start | bytes 12582916
